TPU v7x, 256 devices: a whole 4x4x8 slice. The times are simulated.
256 devices in a mesh: row: 16 (over x, y), col: 16 (over z, core).
Axes of the slice: x: 4, y: 4, z: 8, core: 2. Of those that a mesh axis runs over, the one named last changes fastest.
Arguments:
- image_embed: float32 [12288, 768], P(('row', 'col')), may hold values from -40 to 40, as said below
- text_embed: float32 [12288, 768], P(('col', 'row')), may hold values from -40 to 40, as said below
- logit_scale: float32 [1], replicated, may hold values from 120 to 250
Outputs:
- loss: float32 [], replicated
- grad_image: float32 [12288, 768], P(('row', 'col'))
- grad_text: float32 [12288, 768], P(('col', 'row'))
Inputs may be any that keep to these rules, and one draw needn't show every extreme that they name: Rows of image_embed have norms spread over a factor of ten; text row i is correlated with image row i, and some pairs point the same way. `text_embed`: some text rows nearly repeat the direction of the row before them.
All inputs are finite; a program needn't handle non-finite values.
Results may differ from a plain program's by a relative error of at most 0.0082.
Values may be sent and summed in bfloat16 or wider, within the bound.
A program may use at most 64 MiB of HBM per device.

v0:
```python
import jax
import jax.numpy as jnp
from jax import lax
from jax.sharding import PartitionSpec as P

eps = 1e-06


def body(image_embed, text_embed, logit_scale):
    scale = logit_scale[0]
    row_index = lax.axis_index("row")
    col_index = lax.axis_index("col")
    shard_len = image_embed.shape[0]
    width = image_embed.shape[1]
    batch_total = shard_len * lax.axis_size("row") * lax.axis_size("col")
    inv_image = lax.rsqrt(jnp.sum(image_embed * image_embed, axis=1, keepdims=True) + eps)
    inv_text = lax.rsqrt(jnp.sum(text_embed * text_embed, axis=1, keepdims=True) + eps)
    unit_image = image_embed * inv_image
    unit_text = text_embed * inv_text
    image_block = lax.all_gather(unit_image.astype(jnp.bfloat16), "col", axis=0, tiled=True)
    text_block = lax.all_gather(unit_text.astype(jnp.bfloat16), "row", axis=0, tiled=True)
    image_count = image_block.shape[0]
    text_count = text_block.shape[0]
    count = image_count // image_count
    image_blocks = image_block.reshape(count, image_count, width)
    starts = jnp.arange(count) * image_count
    row_base = row_index * image_count
    col_ids = col_index * text_count + jnp.arange(text_count)

    def logits_of(block):
        return scale * lax.dot_general(
            block, text_block, (((1,), (1,)), ((), ())), preferred_element_type=jnp.float32
        )

    def forward(carry, inputs):
        col_max, col_sum, diag_sum = carry
        block, first = inputs
        logits = logits_of(block)
        local_max = jnp.max(logits, axis=1)
        local_sum = jnp.sum(jnp.exp(logits - local_max[:, None]), axis=1)
        new_max = jnp.maximum(col_max, jnp.max(logits, axis=0))
        col_sum = col_sum * jnp.exp(col_max - new_max) + jnp.sum(
            jnp.exp(logits - new_max[None, :]), axis=0
        )
        row_ids = row_base + first + jnp.arange(image_count)
        delta = row_ids[:, None] == col_ids[None, :]
        diag_sum = diag_sum + jnp.sum(jnp.where(delta, logits, 0.0))
        return ((new_max, col_sum, diag_sum), (local_max, local_sum))

    init = (
        jnp.full((text_count,), -jnp.inf, jnp.float32),
        jnp.zeros((text_count,), jnp.float32),
        jnp.zeros((), jnp.float32),
    )
    (col_max, col_sum, diag_sum), (row_max, row_sum) = lax.scan(
        forward, init, (image_blocks, starts)
    )
    row_max = row_max.reshape(image_count)
    row_sum = row_sum.reshape(image_count)
    row_top = lax.pmax(row_max, "col")
    row_total = lax.psum(row_sum * jnp.exp(row_max - row_top), "col")
    col_top = lax.pmax(col_max, "row")
    col_total = lax.psum(col_sum * jnp.exp(col_max - col_top), "row")
    row_lse = row_top + jnp.log(row_total)
    col_lse = col_top + jnp.log(col_total)
    own_rows = lax.dynamic_slice_in_dim(row_lse, col_index * shard_len, shard_len, 0)
    own_cols = lax.dynamic_slice_in_dim(col_lse, row_index * shard_len, shard_len, 0)
    local_loss = jnp.sum(own_rows) + jnp.sum(own_cols) - 2.0 * diag_sum
    loss = lax.psum(local_loss, ("row", "col")) / (2.0 * batch_total)

    def backward(grad_text, inputs):
        block, first, lse_rows = inputs
        logits = logits_of(block)
        row_ids = row_base + first + jnp.arange(image_count)
        delta = (row_ids[:, None] == col_ids[None, :]).astype(jnp.float32)
        dlogits = (
            (jnp.exp(logits - lse_rows[:, None]) + jnp.exp(logits - col_lse[None, :]) - 2.0 * delta)
            * 0.5
        ).astype(jnp.bfloat16)
        grad_rows = scale * jnp.dot(dlogits, text_block, preferred_element_type=jnp.float32)
        grad_text = grad_text + scale * lax.dot_general(
            dlogits, block, (((0,), (0,)), ((), ())), preferred_element_type=jnp.float32
        )
        return (grad_text, grad_rows)

    text_terms, image_terms = lax.scan(
        backward,
        jnp.zeros((text_count, width), jnp.float32),
        (image_blocks, starts, row_lse.reshape(count, image_count)),
    )
    image_terms = image_terms.reshape(image_count, width)
    image_whole = lax.psum(image_terms, "col")
    text_whole = lax.psum(text_terms, "row")
    grad_unit_image = lax.dynamic_slice_in_dim(image_whole, col_index * shard_len, shard_len, 0)
    grad_unit_text = lax.dynamic_slice_in_dim(text_whole, row_index * shard_len, shard_len, 0)
    grad_image = inv_image * (
        grad_unit_image - unit_image * jnp.sum(unit_image * grad_unit_image, axis=1, keepdims=True)
    )
    grad_text = inv_text * (
        grad_unit_text - unit_text * jnp.sum(unit_text * grad_unit_text, axis=1, keepdims=True)
    )
    return (loss, grad_image, grad_text)


def solution(mesh):
    placed = (P(("row", "col"), None), P(("col", "row"), None), P())
    return jax.shard_map(
        body,
        mesh=mesh,
        in_specs=placed,
        out_specs=(P(), P(("row", "col"), None), P(("col", "row"), None)),
        check_vma=False,
    )
```

profile of v0, /device:TPU:1, one launch (start us, length us, event | category | flops | bytes accessed | tf_op | source)
XLA Modules:
  0.0 462.6 jit_solution(8368033194433236928)
XLA Ops:
  7.2 0.0 all-gather.5.cloned.1.call-start
  7.2 1.0 multiply_reduce_fusion.2
  8.2 1.6 multiply_convert_fusion
  9.9 0.0 all-gather.5.cloned.1.call-update
  9.9 0.0 all-gather.3.cloned.1.call-start
  10.0 1.0 multiply_reduce_fusion.3
  11.0 1.6 multiply_convert_fusion.1
  12.6 0.0 all-gather.3.cloned.1.call-update
  12.6 0.0 all-reduce.3.cloned.1.call-start
  13.4 48.8 %all-gather.5.cloned.1.call-done = bf16[768,768]{1,0:T(8,128)(2,1)} async-done(((bf16[48,768]{1,0:T(8,128)(2,1)}), bf16[768,768]{1,0:T(8,128)(2,1)}) %all-gather.5.cloned.1.call-update) | async-done | bytes 1179664 | tf_op jit(solution)/shard_map/all_gather | solution.py:21
  62.1 42.0 %all-gather.3.cloned.1.call-done = bf16[768,768]{1,0:T(8,128)(2,1)} async-done(((bf16[48,768]{1,0:T(8,128)(2,1)}), bf16[768,768]{1,0:T(8,128)(2,1)}) %all-gather.3.cloned.1.call-update) | async-done | bytes 1179664 | tf_op jit(solution)/shard_map/all_gather | solution.py:20
  104.1 2.8 fusion.6
  106.9 33.2 %pmax.15 = f32[768]{0:T(1024)S(1)} all-reduce(f32[768]{0:T(1024)S(1)} %get-tuple-element.49), channel_id=1, replica_groups=mesh['row'=16,'col'=16] {'row'}, use_global_device_ids=true, to_apply=%region_8.9 | all-reduce | flops 768 | bytes 6144 | tf_op jit(solution)/shard_map/pmax | solution.py:62
  140.1 30.3 %pmax.14 = f32[768]{0:T(1024)S(1)} all-reduce(f32[768]{0:T(1024)S(1)} %get-tuple-element.50), channel_id=1, replica_groups=mesh['row'=16,'col'=16] {'col'}, use_global_device_ids=true, to_apply=%region_3.4 | all-reduce | flops 768 | bytes 6144 | tf_op jit(solution)/shard_map/pmax | solution.py:60
  170.4 2.1 fusion
  172.5 28.5 %psum.36 = f32[768]{0:T(1024)S(1)} all-reduce(f32[768]{0:T(1024)S(1)} %exponential_multiply_fusion), channel_id=1, replica_groups=mesh['row'=16,'col'=16] {'row'}, use_global_device_ids=true, to_apply=%region_10.11 | all-reduce | flops 768 | bytes 6144 | tf_op jit(solution)/shard_map/psum | solution.py:63
  201.0 30.5 %psum.35 = f32[768]{0:T(1024)S(1)} all-reduce(f32[768]{0:T(1024)S(1)} %exponential_multiply_fusion.1), channel_id=1, replica_groups=mesh['row'=16,'col'=16] {'col'}, use_global_device_ids=true, to_apply=%region_5.6 | all-reduce | flops 768 | bytes 6144 | tf_op jit(solution)/shard_map/psum | solution.py:61
  231.5 4.5 convolution_multiply_fusion.1
  236.0 0.0 all-reduce.3.cloned.1.call-update
  236.0 0.0 all-reduce.5.cloned.1.call-start
  236.0 4.4 convolution_multiply_fusion
  240.5 0.0 all-reduce.5.cloned.1.call-update
  240.5 0.7 dynamic-slice_reduce_fusion
  241.2 0.7 dynamic-slice_reduce_fusion.1
  243.8 73.8 %psum.37 = f32[]{:T(128)} all-reduce(f32[]{:T(128)S(6)} %sub.78), channel_id=1, replica_groups=mesh['row'=16,'col'=16] {'row','col'}, use_global_device_ids=true, to_apply=%region_13.14 | all-reduce | flops 1 | bytes 8 | tf_op jit(solution)/shard_map/psum | solution.py:69
  318.2 29.4 %all-reduce.3.cloned.1.call-done = f32[768,768]{1,0:T(8,128)} async-done(((f32[768,768]{1,0:T(8,128)}), f32[768,768]{1,0:T(8,128)}) %all-reduce.3.cloned.1.call-update) | async-done | bytes 2359312 | tf_op jit(solution)/shard_map/psum | solution.py:92
  347.6 0.0 copy-done
  347.6 1.1 multiply_reduce_fusion.1
  348.7 1.7 subtract_multiply_fusion.1
  350.4 101.8 %all-reduce.5.cloned.1.call-done = f32[768,768]{1,0:T(8,128)} async-done(((f32[768,768]{1,0:T(8,128)}), f32[768,768]{1,0:T(8,128)}) %all-reduce.5.cloned.1.call-update) | async-done | bytes 2359312 | tf_op jit(solution)/shard_map/psum | solution.py:93
  452.2 1.1 multiply_reduce_fusion
  453.3 1.7 subtract_multiply_fusion
  (10 shorter events, 0.1 us)
Async XLA Ops:
  7.2 55.0 %all-gather.5.cloned.1.call-start = ((), (), s32[]{:S(2)}) async-start(), calls=%async_computation.1 | async-start | bytes 1253376 | tf_op jit(solution)/shard_map/all_gather | solution.py:21
  9.9 94.2 %all-gather.3.cloned.1.call-start = ((), (), s32[]{:S(2)}) async-start(), calls=%async_computation | async-start | bytes 1253376 | tf_op jit(solution)/shard_map/all_gather | solution.py:20
  12.6 335.0 %all-reduce.3.cloned.1.call-start = ((), (), s32[]{:S(2)}) async-start(), calls=%async_computation.2 | async-start | bytes 4718592 | tf_op jit(solution)/shard_map/psum | solution.py:92
  236.0 216.2 %all-reduce.5.cloned.1.call-start = ((), (), s32[]{:S(2)}) async-start(), calls=%async_computation.3 | async-start | bytes 4718592 | tf_op jit(solution)/shard_map/psum | solution.py:93
  240.5 107.2 %copy-start = (f32[48,768]{1,0:T(8,128)S(1)}, f32[48,768]{1,0:T(8,128)}, u32[]{:S(2)}) copy-start(f32[48,768]{1,0:T(8,128)} %param.3) | copy-start | bytes 442372
  240.5 211.7 %copy-start.1 = (f32[48,768]{1,0:T(8,128)S(1)}, f32[48,768]{1,0:T(8,128)}, u32[]{:S(2)}) copy-start(f32[48,768]{1,0:T(8,128)} %param.4) | copy-start | bytes 442372
Sparse Core Ops, SparseCore 0:
  11.0 51.0 all-gather.4
  64.5 39.5 all-gather.2
  236.1 111.4 all-reduce.2
  350.8 101.2 all-reduce.4
where the time goes:
time: 463 us
  waiting for transfers between devices  222 us (48%)
  blocking collectives  196 us (42%)
  between operations  18.2 us (4%)
  other arithmetic  14.3 us (3%)
  matrix products  11.7 us (3%)
    psum x1, waiting for transfers between devices, body(): text_whole = lax.psum(text_terms, 'row')  102 us
    psum x1, blocking collectives, body(): loss = lax.psum(local_loss, ('row', 'col')) / (2.0 * batch_total)  73.8 us
    all_gather x1, waiting for transfers between devices, body(): lax.all_gather(unit_text.astype(jnp.bfloat16), 'row', axis=0, tiled=True)  48.8 us
    all_gather x1, waiting for transfers between devices, body(): lax.all_gather(unit_image.astype(jnp.bfloat16), 'col', axis=0, tiled=True)  42 us
    pmax x1, blocking collectives, body(): col_top = lax.pmax(col_max, 'row')  33.2 us
    psum x1, blocking collectives, body(): row_total = lax.psum(row_sum * jnp.exp(row_max - row_top), 'col')  30.5 us
    pmax x1, blocking collectives, body(): row_top = lax.pmax(row_max, 'col')  30.3 us
    psum x1, waiting for transfers between devices, body(): image_whole = lax.psum(image_terms, 'col')  29.4 us
  transfers between devices with their start and end apart: 4, of which 4 were waited for; matrix products, arithmetic and copies ran while one was open for 2% of the time, Pallas kernels for 0%

commit v1 on v0

v1 whole, which is shorter than its diff:
```python
import jax
import jax.numpy as jnp
from jax import lax
from jax.experimental import pallas as pl
from jax.experimental.pallas import tpu as pltpu
from jax.sharding import PartitionSpec as P

EPS = 1e-06
LOG2E = 1.4426950408889634
LN2 = 0.6931471805599453
MESH = pl.DeviceIdType.MESH
F32 = jnp.float32
BF16 = jnp.bfloat16
SHARD, WIDTH, BLOCK, TILE = 48, 768, 768, 128
TILES = BLOCK // TILE
HALF = WIDTH // 2
ROWS, COLS, ZS = 16, 16, 8


def kernel(
    image_hbm, text_hbm, scale_ref, loss_ref, grad_image_ref, grad_text_ref,
    image_in, text_in, image_all, text_all, logits, col_parts, dlogits,
    row_stats, col_stats, row_loss, col_loss,
    image_part, image_other, image_sum, image_hop, image_far, image_half, image_near,
    text_part, text_line, text_hop, text_near,
    in_sem, gather_send, gather_recv, stat_send, stat_recv, reduce_send, reduce_recv,
):
    r = lax.axis_index("row")
    c = lax.axis_index("col")
    x, y = r // 4, r % 4
    z, k = c // 2, c % 2
    a_pos, b_pos = x + k * (y - x), y + k * (x - y)
    a_step, b_step = 4 - 3 * k, 1 + 3 * k

    def line(a, b):
        return a * a_step + b * b_step

    def up(d):
        return (r, ((z + d + ZS) % ZS) * 2 + k)

    def copy(src, dst, send, recv, device):
        return pltpu.make_async_remote_copy(
            src_ref=src, dst_ref=dst, send_sem=send, recv_sem=recv,
            device_id=device, device_id_type=MESH,
        )

    loads = [
        pltpu.make_async_copy(image_hbm, image_in, in_sem.at[0]),
        pltpu.make_async_copy(text_hbm, text_in, in_sem.at[1]),
    ]
    for load in loads:
        load.start()
    barrier = pltpu.get_barrier_semaphore()
    for i in range(1, 16):
        pl.semaphore_signal(barrier, inc=1, device_id=((r + i) % ROWS, c), device_id_type=MESH)
        pl.semaphore_signal(barrier, inc=1, device_id=(r, (c + i) % COLS), device_id_type=MESH)

    def rows_of(ref, index):
        return ref.at[pl.ds(pl.multiple_of(index * SHARD, SHARD), SHARD), :]

    def normalised(ref):
        rows = ref[...]
        inverse = lax.rsqrt(jnp.sum(rows * rows, axis=1, keepdims=True) + EPS)
        return rows * inverse, inverse

    loads[0].wait()
    rows_of(image_all, c)[...] = normalised(image_in)[0].astype(BF16)
    loads[1].wait()
    rows_of(text_all, r)[...] = normalised(text_in)[0].astype(BF16)
    pl.semaphore_wait(barrier, 30)

    started = []

    def gather(src, index, device):
        cp = copy(src, src, gather_send.at[index], gather_recv.at[index], device)
        cp.start()
        started.append(cp)
        return cp

    def image_rows(d):
        return rows_of(image_all, ((z + d + ZS) % ZS) * 2 + k)

    def half_of(block, which):
        return block.at[:, which * HALF:(which + 1) * HALF]

    sibling = (r, z * 2 + 1 - k)
    text_own = rows_of(text_all, r)
    near = {}
    hops = {}
    for d in (2, -2):
        hops[d] = gather(image_rows(0), 2 + d, up(d))
    for a in (2, 1, 3):
        near[a] = gather(text_own, 16 + a, (line((a_pos + a) % 4, b_pos), c))
    for d in (1, -1):
        hops[d] = gather(image_rows(0), 2 + d, up(d))
    shares = [gather(image_rows(0), 7, sibling)]
    across = []

    def pass_text(a):
        block = rows_of(text_all, line((a_pos + 4 - a) % 4, b_pos))
        for b in (2, 1, 3):
            across.append(gather(block, 20 + 4 * a + b, (line(a_pos, (b_pos + b) % 4), c)))

    pass_text(0)
    ends = []
    for d, sign in ((2, 1), (-2, -1)):
        hops[d].wait_recv()
        block = image_rows(-d)
        ends.append(gather(block, 5 + (sign > 0), up(sign)))
        ends.append(gather(half_of(block, 0 if sign > 0 else 1), 36 + (sign > 0), up(d)))
        shares.append(gather(block, 10 + d, sibling))
    for a in (1, 3, 2):
        near[a].wait_recv()
        pass_text(a)
    for d in (1, -1):
        hops[d].wait_recv()
        shares.append(gather(image_rows(-d), 10 + d, sibling))
    ends[0].wait_recv()
    shares.append(gather(image_rows(-3), 13, sibling))
    ends[2].wait_recv()
    shares.append(gather(image_rows(3), 14, sibling))
    ends[1].wait_recv()
    ends[3].wait_recv()
    shares.append(gather(image_rows(4), 15, sibling))
    for cp in across + shares:
        cp.wait_recv()
    for cp in started:
        cp.wait_send()

    scale = scale_ref[0]
    scale2 = scale * LOG2E
    on_diagonal = (r == c).astype(F32)
    eye = lax.broadcasted_iota(jnp.int32, (TILE, TILE), 0) == lax.broadcasted_iota(
        jnp.int32, (TILE, TILE), 1
    )

    def forward(q, diagonal):
        first = pl.multiple_of(q * TILE, TILE)
        block = scale2 * lax.dot_general(
            image_all[pl.ds(first, TILE), :], text_all[...], (((1,), (1,)), ((), ())),
            preferred_element_type=F32,
        )
        logits[pl.ds(first, TILE), :] = block
        row_max = jnp.max(block, axis=1, keepdims=True)
        row_lse = row_max + jnp.log2(jnp.sum(jnp.exp2(block - row_max), axis=1, keepdims=True))
        col_max = jnp.max(block, axis=0, keepdims=True)
        col_lse = col_max + jnp.log2(jnp.sum(jnp.exp2(block - col_max), axis=0, keepdims=True))
        row_stats[0, pl.ds(q, 1), :] = jnp.broadcast_to(row_lse, (TILE, TILE)).T[0:1, :]
        col_parts[pl.ds(q, 1), :] = col_lse
        own = logits[pl.ds(first, TILE), pl.ds(first, TILE)]
        return diagonal + jnp.sum(jnp.where(eye, own, 0.0), axis=0, keepdims=True)

    diagonal = lax.fori_loop(0, TILES, forward, jnp.zeros((1, TILE), F32))
    row_stats[0, 6:8, :] = jnp.concatenate([diagonal * on_diagonal, jnp.zeros((1, TILE), F32)], axis=0)
    parts = col_parts[0:TILES, :]
    top = jnp.max(parts, axis=0, keepdims=True)
    merged = top + jnp.log2(jnp.sum(jnp.exp2(parts - top), axis=0, keepdims=True))
    for q in range(TILES):
        col_stats[0, q:q + 1, :] = merged[:, q * TILE:(q + 1) * TILE]
    col_stats[0, 6:8, :] = jnp.zeros((2, TILE), F32)

    def exchange(to_cols, to_rows, base):
        copies = []
        for i in range(1, 16):
            copies.append(copy(
                to_cols.at[0], to_cols.at[i], stat_send.at[base + i], stat_recv.at[base + i],
                (r, (c + i) % COLS),
            ))
            copies.append(copy(
                to_rows.at[0], to_rows.at[i], stat_send.at[base + 16 + i],
                stat_recv.at[base + 16 + i], ((r + i) % ROWS, c),
            ))
        for cp in copies:
            cp.start()
        return copies

    copies = exchange(row_stats, col_stats, 0)
    for cp in copies:
        cp.wait_recv()

    def merge(stats):
        every = stats[...]
        most = jnp.max(every, axis=0)
        return most + jnp.log2(jnp.sum(jnp.exp2(every - most[None]), axis=0))

    row_lse = merge(row_stats)
    col_lse = merge(col_stats)
    lse_columns = row_lse.T
    diagonal_sum = jnp.sum(row_stats[...], axis=0)[6:7, :]
    for cp in copies:
        cp.wait_send()

    col_row = jnp.concatenate([col_lse[q:q + 1, :] for q in range(TILES)], axis=1)
    for q in range(TILES):
        rows = slice(q * TILE, (q + 1) * TILE)
        block = logits[rows, :]
        total = jnp.exp2(block - lse_columns[:, q:q + 1]) + jnp.exp2(block - col_row)
        dlogits[rows, :] = (0.5 * total).astype(BF16)
        near_own = total[:, rows] - jnp.where(eye, 2.0 * on_diagonal, 0.0)
        dlogits[rows, rows] = (0.5 * near_own).astype(BF16)

    pending = []

    def reduce(src, dst, index, device):
        cp = copy(src, dst, reduce_send.at[index], reduce_recv.at[index], device)
        cp.start()
        pending.append(cp)
        return cp

    def image_terms(q, carry):
        part = scale * jnp.dot(
            dlogits[pl.ds(pl.multiple_of(q * 192, 192), 192), :], text_all[...],
            preferred_element_type=F32,
        )
        image_part[pl.ds(2 * q, 2)] = part.astype(BF16).reshape(2, 2, SHARD, WIDTH)
        return carry

    lax.fori_loop(0, 4, image_terms, 0)
    swap = reduce(image_part.at[:, 1 - k], image_other, 0, sibling)

    for q in range(3):
        rows = slice(q * 256, (q + 1) * 256)
        part = scale * lax.dot_general(
            dlogits[:, rows], image_all[...], (((0,), (0,)), ((), ())), preferred_element_type=F32
        )
        text_part[rows, :] = part.astype(BF16)

    lines = {}
    for b in (2, 1, 3):
        for a in range(4):
            lines[a, b] = reduce(
                rows_of(text_part, line(a, (b_pos + b) % 4)), text_line.at[b - 1, a],
                16 + 4 * b + a, (line(a_pos, (b_pos + b) % 4), c),
            )

    swap.wait_recv()

    def of_z(d):
        index = (z + d + ZS) % ZS
        return image_part[index, k].astype(F32) + image_other[index].astype(F32)

    def send_sum(d):
        image_sum[d % ZS] = of_z(d).astype(BF16)
        return image_sum.at[d % ZS]

    far = {}
    quarter = {}
    direct = {}
    block = send_sum(4)
    for s, sign in ((0, 1), (1, -1)):
        quarter[sign] = reduce(half_of(block, s), image_half.at[s], 1 + s, up(2 * sign))
    for s, sign in ((0, 1), (1, -1)):
        far[sign] = reduce(send_sum(3 * sign), image_far.at[s], 3 + s, up(sign))
    for s, sign in ((0, 1), (1, -1)):
        direct[sign] = reduce(send_sum(sign), image_near.at[s], 5 + s, up(sign))

    total_row = jnp.sum(row_lse[0:6, :], axis=0, keepdims=True) - 2.0 * diagonal_sum
    total_col = jnp.sum(col_lse[0:6, :], axis=0, keepdims=True)
    row_loss[0] = jnp.broadcast_to(total_row, (8, TILE))
    col_loss[0] = jnp.broadcast_to(total_col, (8, TILE))
    loss_copies = exchange(col_loss, row_loss, 32)

    hop = {}
    for s, sign in ((0, 1), (1, -1)):
        far[sign].wait_recv()
        quarter[sign].wait_recv()
        both = of_z(2 * sign) + image_far[s].astype(F32)
        cols = slice(s * HALF, (s + 1) * HALF)
        other = slice((1 - s) * HALF, (2 - s) * HALF)
        slot = image_sum.at[(2 * sign) % ZS]
        slot[:, other] = both[:, other].astype(BF16)
        slot[:, cols] = (both[:, cols] + image_half[s].astype(F32)).astype(BF16)
        hop[sign] = reduce(slot, image_hop.at[s], 7 + s, up(2 * sign))

    for cp in lines.values():
        cp.wait_recv()

    def of_line(a):
        index = (a_pos + a) % 4
        total = rows_of(text_part, line(index, b_pos))[...].astype(F32)
        for b in range(3):
            total = total + text_line[b, index].astype(F32)
        return total

    last = {}
    for a in (2, 1, 3):
        text_hop[a] = of_line(a).astype(BF16)
        last[a] = reduce(
            text_hop.at[a], text_near.at[a], 8 + a, (line((a_pos + a) % 4, b_pos), c)
        )

    def project(ref, gradient):
        unit, inverse = normalised(ref)
        return inverse * (gradient - unit * jnp.sum(unit * gradient, axis=1, keepdims=True))

    gradient = of_z(0)
    for s, sign in ((0, 1), (1, -1)):
        direct[sign].wait_recv()
        gradient = gradient + image_near[s].astype(F32)
    for s, sign in ((0, 1), (1, -1)):
        hop[sign].wait_recv()
        gradient = gradient + image_hop[s].astype(F32)
    grad_image_ref[...] = project(image_in, gradient)

    gradient = of_line(0)
    for a in (2, 1, 3):
        last[a].wait_recv()
        gradient = gradient + text_near[a].astype(F32)
    grad_text_ref[...] = project(text_in, gradient)

    for cp in loss_copies:
        cp.wait_recv()
    sums = jnp.sum(row_loss[...] + col_loss[...], axis=0)[0:1, :]
    loss_ref[...] = jnp.broadcast_to(
        jnp.sum(sums, axis=1, keepdims=True) * (LN2 / (2.0 * ROWS * BLOCK)), (1, TILE)
    )
    for cp in pending + loss_copies:
        cp.wait_send()


def body(image_embed, text_embed, logit_scale):
    loss, grad_image, grad_text = pl.pallas_call(
        kernel,
        name="contrastive",
        out_shape=(
            jax.ShapeDtypeStruct((1, TILE), F32),
            jax.ShapeDtypeStruct((SHARD, WIDTH), F32),
            jax.ShapeDtypeStruct((SHARD, WIDTH), F32),
        ),
        in_specs=[
            pl.BlockSpec(memory_space=pl.ANY),
            pl.BlockSpec(memory_space=pl.ANY),
            pl.BlockSpec(memory_space=pltpu.SMEM),
        ],
        out_specs=(pl.BlockSpec(memory_space=pltpu.VMEM),) * 3,
        scratch_shapes=[
            pltpu.VMEM((SHARD, WIDTH), F32),
            pltpu.VMEM((SHARD, WIDTH), F32),
            pltpu.VMEM((BLOCK, WIDTH), BF16),
            pltpu.VMEM((BLOCK, WIDTH), BF16),
            pltpu.VMEM((BLOCK, BLOCK), F32),
            pltpu.VMEM((8, BLOCK), F32),
            pltpu.VMEM((BLOCK, BLOCK), BF16),
            pltpu.VMEM((16, 8, TILE), F32),
            pltpu.VMEM((16, 8, TILE), F32),
            pltpu.VMEM((16, 8, TILE), F32),
            pltpu.VMEM((16, 8, TILE), F32),
            pltpu.VMEM((ZS, 2, SHARD, WIDTH), BF16),
            pltpu.VMEM((ZS, SHARD, WIDTH), BF16),
            pltpu.VMEM((ZS, SHARD, WIDTH), BF16),
            pltpu.VMEM((2, SHARD, WIDTH), BF16),
            pltpu.VMEM((2, SHARD, WIDTH), BF16),
            pltpu.VMEM((2, SHARD, HALF), BF16),
            pltpu.VMEM((2, SHARD, WIDTH), BF16),
            pltpu.VMEM((BLOCK, WIDTH), BF16),
            pltpu.VMEM((3, 4, SHARD, WIDTH), BF16),
            pltpu.VMEM((4, SHARD, WIDTH), BF16),
            pltpu.VMEM((4, SHARD, WIDTH), BF16),
            pltpu.SemaphoreType.DMA((2,)),
            pltpu.SemaphoreType.DMA((40,)),
            pltpu.SemaphoreType.DMA((40,)),
            pltpu.SemaphoreType.DMA((64,)),
            pltpu.SemaphoreType.DMA((64,)),
            pltpu.SemaphoreType.DMA((32,)),
            pltpu.SemaphoreType.DMA((32,)),
        ],
        compiler_params=pltpu.CompilerParams(
            collective_id=0, has_side_effects=True, vmem_limit_bytes=48 << 20
        ),
    )(image_embed, text_embed, logit_scale)
    return loss[0, 0], grad_image, grad_text


def solution(mesh):
    placed = (P(("row", "col"), None), P(("col", "row"), None), P())
    return jax.shard_map(
        body,
        mesh=mesh,
        in_specs=placed,
        out_specs=(P(), P(("row", "col"), None), P(("col", "row"), None)),
        check_vma=False,
    )
```

time: 463 us -> 60.7 us (0.13)
  waiting for transfers between devices: 222 us -> 0 us
  blocking collectives: 196 us -> 0 us
  Pallas kernels: 0 us -> 55 us
  between operations: 18.2 us -> 2.46 us
  other arithmetic: 14.3 us -> 0 us
  matrix products: 11.7 us -> 0 us
    psum x3 -> x0, blocking collectives: 133 us -> none  [the longest x1 73.8 us: body(): loss = lax.psum(local_loss, ('row', 'col')) / (2.0 * batch_total)]
    psum x2 -> x0, waiting for transfers between devices: 131 us -> none  [the longest x1 102 us: body(): text_whole = lax.psum(text_terms, 'row')]
    all_gather x2 -> x0, waiting for transfers between devices: 90.7 us -> none  [the longest x1 48.8 us: body(): lax.all_gather(unit_text.astype(jnp.bfloat16), 'row', axis=0, tiled=True)]
    pmax x2 -> x0, blocking collectives: 63.5 us -> none  [the longest x1 33.2 us: body(): col_top = lax.pmax(col_max, 'row')]
    pallas_call x0 -> x1, Pallas kernels: none -> 55 us  [body(): pl.pallas_call(kernel, name='contrastive', out_shape=(jax.ShapeDtypeStruc...]
    dot_general x3 -> x0, matrix products: 11.7 us -> none  [the longest x1 4.45 us: backward(): jnp.dot(dlogits, text_block, preferred_element_type=jnp.float32)]
    reduce_sum x7 -> x0, other arithmetic: 7.69 us -> none  [the longest x1 2.09 us: forward(): diag_sum = diag_sum + jnp.sum(jnp.where(delta, logits, 0.0))]
  transfers between devices with their start and end apart: 4 -> 0, of which waited for: 4 -> 0; matrix products, arithmetic and copies ran while one was open for 2% -> 0% of each run, Pallas kernels for 0% -> 0%
where the time goes in v1:
time: 60.7 us; the launch traced here: 60.6 us
  Pallas kernels  55 us (91%)
  local copies, waits for them, and re-layouts  3.14 us (5%)
  between operations  2.46 us (4%)
    pallas_call x1, Pallas kernels, body(): pl.pallas_call(kernel, name='contrastive', out_shape=(jax.ShapeDtypeStruc...  55 us
    unnamed x6, local copies, waits for them, and re-layouts  3.14 us

profile of v1, /device:TPU:1, one launch (start us, length us, event | category | flops | bytes accessed | tf_op | source)
XLA Modules:
  0.0 60.6 jit_solution(12950589124162367637)
XLA Ops:
  1.3 0.0 copy-start
  1.3 0.9 %copy-done = f32[48,768]{1,0:T(8,128)S(1)} copy-done((f32[48,768]{1,0:T(8,128)S(1)}, f32[48,768]{1,0:T(8,128)}, u32[]{:S(2)}) %copy-start) | copy-done | bytes 147480
  2.2 0.0 copy-start.1
  2.2 0.9 %copy-done.1 = f32[48,768]{1,0:T(8,128)S(1)} copy-done((f32[48,768]{1,0:T(8,128)S(1)}, f32[48,768]{1,0:T(8,128)}, u32[]{:S(2)}) %copy-start.1) | copy-done | bytes 147480
  3.1 55.0 %contrastive.1 = (f32[1,128]{1,0:T(1,128)S(1)}, f32[48,768]{1,0:T(8,128)S(1)}, f32[48,768]{1,0:T(8,128)S(1)}) custom-call(f32[48,768]{1,0:T(8,128)S(1)} %copy-done, f32[48,768]{1,0:T(8,128)S(1)} %copy-done.1, f32[1]{0:T(128)S(6)} %copy.9.scale_ref), custom_call_target="tpu_custom_call" | custom-call | tf_op jit(solution)/shard_map/contrastive/pallas_call | solution.py:322
  58.1 0.7 %copy.11 = f32[48,768]{1,0:T(8,128)} copy(f32[48,768]{1,0:T(8,128)S(1)} %get-tuple-element.13) | data formatting | bytes 294912
  58.8 0.7 %copy.12 = f32[48,768]{1,0:T(8,128)} copy(f32[48,768]{1,0:T(8,128)S(1)} %get-tuple-element.14) | data formatting | bytes 294912
Async XLA Ops:
  1.3 0.9 %copy-start = (f32[48,768]{1,0:T(8,128)S(1)}, f32[48,768]{1,0:T(8,128)}, u32[]{:S(2)}) copy-start(f32[48,768]{1,0:T(8,128)} %image_hbm.1) | copy-start | bytes 442372
  2.2 0.9 %copy-start.1 = (f32[48,768]{1,0:T(8,128)S(1)}, f32[48,768]{1,0:T(8,128)}, u32[]{:S(2)}) copy-start(f32[48,768]{1,0:T(8,128)} %text_hbm.1) | copy-start | bytes 442372

commit v2 on v1

v2 whole, which is shorter than its diff:
```python
import jax
import jax.numpy as jnp
from jax import lax
from jax.experimental import pallas as pl
from jax.experimental.pallas import tpu as pltpu
from jax.sharding import PartitionSpec as P

EPS = 1e-06
LOG2E = 1.4426950408889634
LN2 = 0.6931471805599453
MESH = pl.DeviceIdType.MESH
F32 = jnp.float32
BF16 = jnp.bfloat16
SHARD, WIDTH, BLOCK, LANES = 48, 768, 768, 128
PAIR = 2 * SHARD
HALF = WIDTH // 2
ROWS, COLS, ZS = 16, 16, 8
ORDER = (4, 3, -3, 2, -2, 1, -1, 0)
SLOT = {d: s for s, d in enumerate(ORDER)} | {-4: 0}


def kernel(
    image_hbm, text_hbm, scale_ref, loss_ref, grad_image_ref, grad_text_ref,
    image_unit, text_unit, image_inv, text_inv, image_all, text_all, logits, col_parts, dlogits,
    row_stats, col_stats, row_merged, loss_a, loss_b,
    image_part, image_other, image_sum, image_hop, image_far, image_half, image_near,
    text_part, text_line, text_hop, text_near,
    in_sem, gather_send, gather_recv, stat_sem, reduce_send, reduce_recv,
):
    r = lax.axis_index("row")
    c = lax.axis_index("col")
    x, y = r // 4, r % 4
    z, k = c // 2, c % 2
    a_pos, b_pos = x + k * (y - x), y + k * (x - y)
    a_step, b_step = 4 - 3 * k, 1 + 3 * k

    def line(a, b):
        return a * a_step + b * b_step

    def on_a(a):
        return (line((a_pos + a) % 4, b_pos), c)

    def on_b(b):
        return (line(a_pos, (b_pos + b) % 4), c)

    def up(d):
        return (r, ((z + d + ZS) % ZS) * 2 + k)

    sibling = (r, z * 2 + 1 - k)

    def copy(src, dst, send, recv, device):
        return pltpu.make_async_remote_copy(
            src_ref=src, dst_ref=dst, send_sem=send, recv_sem=recv,
            device_id=device, device_id_type=MESH,
        )

    loads = [
        pltpu.make_async_copy(image_hbm, image_unit, in_sem.at[0]),
        pltpu.make_async_copy(text_hbm, text_unit, in_sem.at[1]),
    ]
    for load in loads:
        load.start()
    barrier = pltpu.get_barrier_semaphore()
    partners = [up(d) for d in (2, -2, 1, -1)] + [sibling]
    partners += [on_a(a) for a in (1, 2, 3)] + [on_b(b) for b in (1, 2, 3)]
    for device in partners:
        pl.semaphore_signal(barrier, inc=1, device_id=device, device_id_type=MESH)

    def text_rows(index):
        return text_all.at[pl.ds(pl.multiple_of(index * SHARD, SHARD), SHARD), :]

    def image_rows(d):
        first = SLOT[d] * PAIR + k * SHARD
        return image_all.at[pl.ds(pl.multiple_of(first, SHARD), SHARD), :]

    def normalise(ref, inv_ref):
        rows = ref[...]
        inverse = lax.rsqrt(jnp.sum(rows * rows, axis=1, keepdims=True) + EPS)
        unit = rows * inverse
        ref[...] = unit
        inv_ref[...] = jnp.broadcast_to(inverse, (SHARD, LANES))
        return unit.astype(BF16)

    loads[0].wait()
    image_rows(0)[...] = normalise(image_unit, image_inv)
    loads[1].wait()
    text_rows(r)[...] = normalise(text_unit, text_inv)
    row_stats[0] = jnp.zeros((8, LANES), F32)
    col_stats[0] = jnp.zeros((8, LANES), F32)
    pl.semaphore_wait(barrier, len(partners))

    started = []

    def gather(src, dst, index, device):
        cp = copy(src, dst, gather_send.at[index], gather_recv.at[index], device)
        cp.start()
        started.append(cp)
        return cp

    def half_of(block, which):
        return block.at[:, which * HALF:(which + 1) * HALF]

    def share(d, index):
        return gather(image_rows(d), image_rows(d), index, sibling)

    text_own = text_rows(r)
    near = {}
    hops = {}
    across = []
    for d in (2, -2):
        hops[d] = gather(image_rows(0), image_rows(-d), 2 + d, up(d))
    for a in (2, 1, 3):
        near[a] = gather(text_own, text_own, 16 + a, on_a(a))
    for d in (1, -1):
        hops[d] = gather(image_rows(0), image_rows(-d), 2 + d, up(d))
    shares = [share(0, 7)]

    def pass_text(a):
        block = text_rows(line((a_pos + 4 - a) % 4, b_pos))
        for b in (2, 1, 3):
            across.append(gather(block, block, 20 + 4 * a + b, on_b(b)))

    pass_text(0)
    ends = []
    for d, sign in ((2, 1), (-2, -1)):
        hops[d].wait_recv()
        block = image_rows(-d)
        ends.append(gather(block, image_rows(-d - sign), 5 + (sign > 0), up(sign)))
        s = 0 if sign > 0 else 1
        ends.append(gather(half_of(block, s), half_of(image_rows(4), s), 36 + s, up(d)))
        shares.append(share(-d, 10 + d))
    for a in (1, 3, 2):
        near[a].wait_recv()
        pass_text(a)
    for d in (1, -1):
        hops[d].wait_recv()
        shares.append(share(-d, 10 + d))
    ends[0].wait_recv()
    shares.append(share(-3, 13))
    ends[2].wait_recv()
    shares.append(share(3, 14))
    ends[1].wait_recv()
    ends[3].wait_recv()
    shares.append(share(4, 15))
    for cp in across + shares:
        cp.wait_recv()

    scale2 = scale_ref[0] * LOG2E
    apart = lax.broadcasted_iota(jnp.int32, (PAIR, BLOCK), 1) - lax.broadcasted_iota(
        jnp.int32, (PAIR, BLOCK), 0
    )
    lane = lax.broadcasted_iota(jnp.int32, (PAIR, LANES), 1)
    off_diagonal = (r != c).astype(jnp.int32) * (2 * BLOCK)

    def z_of(d):
        return (z + d + ZS) % ZS

    def own_pairs(s):
        return apart == z_of(ORDER[s]) * PAIR + off_diagonal

    row_lse = jnp.zeros((PAIR, LANES), F32)
    diagonal = jnp.zeros((1, BLOCK), F32)
    for h in range(2):
        rows = slice(h * HALF, (h + 1) * HALF)
        logits[rows, :] = scale2 * lax.dot_general(
            image_all[rows, :], text_all[...], (((1,), (1,)), ((), ())),
            preferred_element_type=F32,
        )
        for s in range(4 * h, 4 * h + 4):
            block = logits[s * PAIR:(s + 1) * PAIR, :]
            row_max = jnp.max(block, axis=1, keepdims=True)
            row_sum = jnp.sum(jnp.exp2(block - row_max), axis=1, keepdims=True)
            row_lse = jnp.where(lane == s, row_max + jnp.log2(row_sum), row_lse)
            col_max = jnp.max(block, axis=0, keepdims=True)
            col_sum = jnp.sum(jnp.exp2(block - col_max), axis=0, keepdims=True)
            col_parts[s:s + 1, :] = col_max + jnp.log2(col_sum)
    row_lse = row_lse.T
    for s in range(ZS):
        row_stats[0, pl.ds(z_of(ORDER[s]), 1), 0:PAIR] = row_lse[s:s + 1, :]
    parts = col_parts[...]
    top = jnp.max(parts, axis=0, keepdims=True)
    merged = top + jnp.log2(jnp.sum(jnp.exp2(parts - top), axis=0, keepdims=True))
    for q in range(6):
        col_stats[0, q:q + 1, :] = merged[:, q * LANES:(q + 1) * LANES]

    def col_peer(i):
        return (r, (c + i) % COLS)

    def row_peer(i):
        return ((r + i) % ROWS, c)

    def spread(ref, sem, peer):
        for i in range(1, 16):
            copy(ref.at[0], ref.at[i], stat_sem.at[2 * sem], stat_sem.at[2 * sem + 1], peer(i)).start()

    def others(ref, sem):
        return pltpu.make_async_copy(ref.at[1:16], ref.at[1:16], stat_sem.at[sem])

    spread(row_stats, 0, col_peer)
    spread(col_stats, 1, row_peer)
    for s in range(ZS):
        block = logits[s * PAIR:(s + 1) * PAIR, :]
        diagonal = diagonal + jnp.sum(jnp.where(own_pairs(s), block, 0.0), axis=0, keepdims=True)
    others(row_stats, 1).wait()
    others(col_stats, 3).wait()

    def merge(stats):
        every = stats[...]
        most = jnp.max(every, axis=0)
        return most + jnp.log2(jnp.sum(jnp.exp2(every - most[None]), axis=0))

    row_merged[...] = merge(row_stats)
    col_lse = merge(col_stats)
    ordered = jnp.concatenate([row_merged[pl.ds(z_of(d), 1), :] for d in ORDER], axis=0)
    lse_columns = ordered.T
    col_row = jnp.concatenate([col_lse[q:q + 1, :] for q in range(6)], axis=1)

    pending = []

    def reduce(src, dst, index, device):
        cp = copy(src, dst, reduce_send.at[index], reduce_recv.at[index], device)
        cp.start()
        pending.append(cp)
        return cp

    swaps = []
    for t in range(4):
        for s in (2 * t, 2 * t + 1):
            rows = slice(s * PAIR, (s + 1) * PAIR)
            block = logits[rows, :]
            total = jnp.exp2(block - lse_columns[0:PAIR, s:s + 1]) + jnp.exp2(block - col_row)
            total = total - jnp.where(own_pairs(s), 2.0, 0.0)
            dlogits[rows, :] = (0.5 * total).astype(BF16)
        part = jnp.dot(
            dlogits[2 * t * PAIR:(2 * t + 2) * PAIR, :], text_all[...], preferred_element_type=F32
        )
        image_part[2 * t:2 * t + 2] = part.astype(BF16).reshape(2, 2, SHARD, WIDTH)
        swaps.append(reduce(
            image_part.at[2 * t:2 * t + 2, 1 - k], image_other.at[2 * t:2 * t + 2], 12 + t, sibling
        ))

    def text_terms(h):
        rows = slice(h * HALF, (h + 1) * HALF)
        part = lax.dot_general(
            dlogits[:, rows], image_all[...], (((0,), (0,)), ((), ())), preferred_element_type=F32
        )
        text_part[rows, :] = part.astype(BF16)

    def of_z(d):
        s = SLOT[d]
        return image_part[s, k].astype(F32) + image_other[s].astype(F32)

    def summed(d):
        image_sum[SLOT[d]] = of_z(d).astype(BF16)
        return image_sum.at[SLOT[d]]

    quarter = {}
    far = {}
    direct = {}
    text_terms(0)
    swaps[0].wait_recv()
    block = summed(4)
    for s, sign in ((0, 1), (1, -1)):
        quarter[sign] = reduce(half_of(block, s), image_half.at[s], 1 + s, up(2 * sign))
    far[1] = reduce(summed(3), image_far.at[0], 3, up(1))
    text_terms(1)
    lines = {}
    for b in (2, 1, 3):
        for a in range(4):
            lines[a, b] = reduce(
                text_rows_of(text_part, line(a, (b_pos + b) % 4)), text_line.at[b - 1, a],
                16 + 4 * b + a, on_b(b),
            )
    swaps[1].wait_recv()
    far[-1] = reduce(summed(-3), image_far.at[1], 4, up(-1))
    swaps[2].wait_recv()
    direct[1] = reduce(summed(1), image_near.at[0], 5, up(1))
    swaps[3].wait_recv()
    direct[-1] = reduce(summed(-1), image_near.at[1], 6, up(-1))

    col_total = jnp.sum(col_lse[0:6, :], axis=0, keepdims=True)
    on_block = jnp.sum(diagonal, axis=1, keepdims=True)
    loss_a[0] = jnp.concatenate(
        [col_total, jnp.broadcast_to(on_block, (1, LANES)), jnp.zeros((6, LANES), F32)], axis=0
    )
    spread(loss_a, 2, col_peer)

    hop = {}
    for s, sign in ((0, 1), (1, -1)):
        far[sign].wait_recv()
        quarter[sign].wait_recv()
        both = of_z(2 * sign) + image_far[s].astype(F32)
        cols = slice(s * HALF, (s + 1) * HALF)
        rest = slice((1 - s) * HALF, (2 - s) * HALF)
        slot = image_sum.at[SLOT[2 * sign]]
        slot[:, rest] = both[:, rest].astype(BF16)
        slot[:, cols] = (both[:, cols] + image_half[s].astype(F32)).astype(BF16)
        hop[sign] = reduce(slot, image_hop.at[s], 7 + s, up(2 * sign))

    for cp in lines.values():
        cp.wait_recv()

    def of_line(a):
        index = (a_pos + a) % 4
        total = text_rows_of(text_part, line(index, b_pos))[...].astype(F32)
        for b in range(3):
            total = total + text_line[b, index].astype(F32)
        return total

    last = {}
    for a in (2, 1, 3):
        text_hop[a] = of_line(a).astype(BF16)
        last[a] = reduce(text_hop.at[a], text_near.at[a], 8 + a, on_a(a))

    others(loss_a, 5).wait()
    sums = jnp.sum(loss_a[...], axis=0)
    row_total = jnp.sum(row_merged[:, 0:PAIR], axis=0, keepdims=True)
    row_total = jnp.sum(row_total, axis=1, keepdims=True) - 2.0 * sums[1:2, 0:1]
    loss_b[0] = jnp.broadcast_to(row_total, (8, LANES))
    spread(loss_b, 3, row_peer)

    def project(unit_ref, inv_ref, gradient):
        unit = unit_ref[...]
        along = jnp.sum(unit * gradient, axis=1, keepdims=True)
        return inv_ref[:, 0:1] * (gradient - unit * along)

    gradient = of_z(0)
    for s, sign in ((0, 1), (1, -1)):
        direct[sign].wait_recv()
        gradient = gradient + image_near[s].astype(F32)
    for s, sign in ((0, 1), (1, -1)):
        hop[sign].wait_recv()
        gradient = gradient + image_hop[s].astype(F32)
    grad_image_ref[...] = project(image_unit, image_inv, gradient)

    gradient = of_line(0)
    for a in (2, 1, 3):
        last[a].wait_recv()
        gradient = gradient + text_near[a].astype(F32)
    grad_text_ref[...] = project(text_unit, text_inv, gradient)

    others(loss_b, 7).wait()
    total = jnp.sum(sums[0:1, :], axis=1, keepdims=True) + jnp.sum(loss_b[...], axis=0)[0:1, 0:1]
    loss_ref[...] = jnp.broadcast_to(total * (LN2 / (2.0 * ROWS * BLOCK)), (1, LANES))
    for cp in started + pending:
        cp.wait_send()
    for sem, ref in enumerate((row_stats, col_stats, loss_a, loss_b)):
        others(ref, 2 * sem).wait()


def text_rows_of(ref, index):
    return ref.at[pl.ds(pl.multiple_of(index * SHARD, SHARD), SHARD), :]


def body(image_embed, text_embed, logit_scale):
    loss, grad_image, grad_text = pl.pallas_call(
        kernel,
        name="contrastive",
        out_shape=(
            jax.ShapeDtypeStruct((1, LANES), F32),
            jax.ShapeDtypeStruct((SHARD, WIDTH), F32),
            jax.ShapeDtypeStruct((SHARD, WIDTH), F32),
        ),
        in_specs=[
            pl.BlockSpec(memory_space=pl.ANY),
            pl.BlockSpec(memory_space=pl.ANY),
            pl.BlockSpec(memory_space=pltpu.SMEM),
        ],
        out_specs=(pl.BlockSpec(memory_space=pltpu.VMEM),) * 3,
        scratch_shapes=[
            pltpu.VMEM((SHARD, WIDTH), F32),
            pltpu.VMEM((SHARD, WIDTH), F32),
            pltpu.VMEM((SHARD, LANES), F32),
            pltpu.VMEM((SHARD, LANES), F32),
            pltpu.VMEM((BLOCK, WIDTH), BF16),
            pltpu.VMEM((BLOCK, WIDTH), BF16),
            pltpu.VMEM((BLOCK, BLOCK), F32),
            pltpu.VMEM((ZS, BLOCK), F32),
            pltpu.VMEM((BLOCK, BLOCK), BF16),
            pltpu.VMEM((16, 8, LANES), F32),
            pltpu.VMEM((16, 8, LANES), F32),
            pltpu.VMEM((8, LANES), F32),
            pltpu.VMEM((16, 8, LANES), F32),
            pltpu.VMEM((16, 8, LANES), F32),
            pltpu.VMEM((ZS, 2, SHARD, WIDTH), BF16),
            pltpu.VMEM((ZS, SHARD, WIDTH), BF16),
            pltpu.VMEM((ZS, SHARD, WIDTH), BF16),
            pltpu.VMEM((2, SHARD, WIDTH), BF16),
            pltpu.VMEM((2, SHARD, WIDTH), BF16),
            pltpu.VMEM((2, SHARD, HALF), BF16),
            pltpu.VMEM((2, SHARD, WIDTH), BF16),
            pltpu.VMEM((BLOCK, WIDTH), BF16),
            pltpu.VMEM((3, 4, SHARD, WIDTH), BF16),
            pltpu.VMEM((4, SHARD, WIDTH), BF16),
            pltpu.VMEM((4, SHARD, WIDTH), BF16),
            pltpu.SemaphoreType.DMA((2,)),
            pltpu.SemaphoreType.DMA((40,)),
            pltpu.SemaphoreType.DMA((40,)),
            pltpu.SemaphoreType.DMA((8,)),
            pltpu.SemaphoreType.DMA((32,)),
            pltpu.SemaphoreType.DMA((32,)),
        ],
        compiler_params=pltpu.CompilerParams(
            collective_id=0, has_side_effects=True, vmem_limit_bytes=60 << 20
        ),
    )(image_embed, text_embed, logit_scale)
    scale = logit_scale[0]
    return loss[0, 0], scale * grad_image, scale * grad_text


def solution(mesh):
    placed = (P(("row", "col"), None), P(("col", "row"), None), P())
    return jax.shard_map(
        body,
        mesh=mesh,
        in_specs=placed,
        out_specs=(P(), P(("row", "col"), None), P(("col", "row"), None)),
        check_vma=False,
    )
```

time: 60.7 us -> 55.7 us (0.918)
  Pallas kernels: 55 us -> 50.7 us
  local copies, waits for them, and re-layouts: 3.14 us -> 0.6 us
  other arithmetic: 0 us -> 1.71 us
    pallas_call x1, Pallas kernels: 55 us -> 50.7 us  [body(): pl.pallas_call(kernel, name='contrastive', out_shape=(jax.ShapeDtypeStruc...]
    unnamed x6 -> x2, local copies, waits for them, and re-layouts: 3.14 us -> 0.6 us
    mul x0 -> x1, other arithmetic: none -> 1.71 us  [body(): return (loss[0, 0], scale * grad_image, scale * grad_text)]
where the time goes in v2:
time: 55.7 us; the launch traced here: 55.5 us
  Pallas kernels  50.7 us (91%)
  between operations  2.45 us (4%)
  other arithmetic  1.71 us (3%)
  local copies, waits for them, and re-layouts  0.6 us (1%)
    pallas_call x1, Pallas kernels, body(): pl.pallas_call(kernel, name='contrastive', out_shape=(jax.ShapeDtypeStruc...  50.7 us
    mul x1, other arithmetic, body(): return (loss[0, 0], scale * grad_image, scale * grad_text)  1.71 us

profile of v2, /device:TPU:1, one launch (start us, length us, event | category | flops | bytes accessed | tf_op | source)
XLA Modules:
  0.0 55.5 jit_solution(15911907007323466539)
XLA Ops:
  1.3 50.7 %contrastive.1 = (f32[1,128]{1,0:T(1,128)}, f32[48,768]{1,0:T(8,128)}, f32[48,768]{1,0:T(8,128)}) custom-call(f32[48,768]{1,0:T(8,128)} %image_hbm.1, f32[48,768]{1,0:T(8,128)} %text_hbm.1, f32[1]{0:T(128)} %copy.7.scale_ref), custom_call_target="tpu_custom_call" | custom-call | tf_op jit(solution)/shard_map/contrastive/pallas_call | solution.py:356
  52.0 1.7 %broadcast_multiply_fusion = (f32[48,768]{1,0:T(8,128)}, f32[48,768]{1,0:T(8,128)}) fusion(f32[48,768]{1,0:T(8,128)} %get-tuple-element.8, f32[]{:T(128)} %bitcast.3, f32[48,768]{1,0:T(8,128)} %get-tuple-element.7), kind=kLoop, calls=%fused_computation | loop fusion | flops 73728 | bytes 589828 | tf_op jit(solution)/shard_map/mul | solution.py:408
  53.7 0.0 copy-start
  53.7 0.6 %copy-done = f32[1,128]{1,0:T(1,128)S(1)} copy-done((f32[1,128]{1,0:T(1,128)S(1)}, f32[1,128]{1,0:T(1,128)}, u32[]{:S(2)}) %copy-start) | copy-done | bytes 536
Async XLA Ops:
  53.7 0.6 %copy-start = (f32[1,128]{1,0:T(1,128)S(1)}, f32[1,128]{1,0:T(1,128)}, u32[]{:S(2)}) copy-start(f32[1,128]{1,0:T(1,128)} %get-tuple-element.6) | copy-start | bytes 1540

commit v3 on v2

--- a/solution.py
+++ b/solution.py
@@ -81,12 +81,10 @@
         inv_ref[...] = jnp.broadcast_to(inverse, (SHARD, LANES))
         return unit.astype(BF16)
 
+    row_stats[0] = jnp.zeros((8, LANES), F32)
+    col_stats[0] = jnp.zeros((8, LANES), F32)
     loads[0].wait()
     image_rows(0)[...] = normalise(image_unit, image_inv)
-    loads[1].wait()
-    text_rows(r)[...] = normalise(text_unit, text_inv)
-    row_stats[0] = jnp.zeros((8, LANES), F32)
-    col_stats[0] = jnp.zeros((8, LANES), F32)
     pl.semaphore_wait(barrier, len(partners))
 
     started = []
@@ -103,17 +101,25 @@
     def share(d, index):
         return gather(image_rows(d), image_rows(d), index, sibling)
 
+    sides = ((0, 1), (1, -1))
+    ahead = {}
+    hops = {}
+    near = {}
+    across = []
+    ends = []
+    for turn in range(2):
+        for s, sign in sides:
+            h = (s + turn) % 2
+            ahead[turn, sign] = gather(
+                half_of(image_rows(0), h), half_of(image_rows(-2 * sign), h), 4 * s + turn, up(2 * sign)
+            )
+    loads[1].wait()
     text_own = text_rows(r)
-    near = {}
-    hops = {}
-    across = []
-    for d in (2, -2):
-        hops[d] = gather(image_rows(0), image_rows(-d), 2 + d, up(d))
-    for a in (2, 1, 3):
+    text_own[...] = normalise(text_unit, text_inv)
+    for a in (1, 3, 2):
         near[a] = gather(text_own, text_own, 16 + a, on_a(a))
-    for d in (1, -1):
-        hops[d] = gather(image_rows(0), image_rows(-d), 2 + d, up(d))
-    shares = [share(0, 7)]
+    for s, sign in sides:
+        hops[sign] = gather(image_rows(0), image_rows(-sign), 4 * s + 2, up(sign))
 
     def pass_text(a):
         block = text_rows(line((a_pos + 4 - a) % 4, b_pos))
@@ -121,31 +127,38 @@
             across.append(gather(block, block, 20 + 4 * a + b, on_b(b)))
 
     pass_text(0)
-    ends = []
-    for d, sign in ((2, 1), (-2, -1)):
-        hops[d].wait_recv()
-        block = image_rows(-d)
-        ends.append(gather(block, image_rows(-d - sign), 5 + (sign > 0), up(sign)))
-        s = 0 if sign > 0 else 1
-        ends.append(gather(half_of(block, s), half_of(image_rows(4), s), 36 + s, up(d)))
-        shares.append(share(-d, 10 + d))
-    for a in (1, 3, 2):
+    shares = [share(0, 8)]
+
+    def pass_image(turn):
+        for s, sign in sides:
+            h = (s + turn) % 2
+            ahead[turn, sign].wait_recv()
+            block = half_of(image_rows(-2 * sign), h)
+            if turn == 0:
+                ends.append(gather(block, half_of(image_rows(4), h), 36 + s, up(2 * sign)))
+            ends.append(gather(block, half_of(image_rows(-3 * sign), h), 38 + 2 * s + turn, up(sign)))
+
+    for a in (1, 3):
         near[a].wait_recv()
         pass_text(a)
-    for d in (1, -1):
-        hops[d].wait_recv()
-        shares.append(share(-d, 10 + d))
-    ends[0].wait_recv()
-    shares.append(share(-3, 13))
-    ends[2].wait_recv()
-    shares.append(share(3, 14))
-    ends[1].wait_recv()
-    ends[3].wait_recv()
-    shares.append(share(4, 15))
+    pass_image(0)
+    near[2].wait_recv()
+    pass_text(2)
+    for s, sign in sides:
+        hops[sign].wait_recv()
+        shares.append(share(-sign, 9 + s))
+    pass_image(1)
+    for s, sign in sides:
+        shares.append(share(-2 * sign, 11 + s))
+    for cp in ends:
+        cp.wait_recv()
+    for d, index in ((3, 13), (-3, 14), (4, 15)):
+        shares.append(share(d, index))
     for cp in across + shares:
         cp.wait_recv()
 
-    scale2 = scale_ref[0] * LOG2E
+    scale = scale_ref[0]
+    scale2 = scale * LOG2E
     apart = lax.broadcasted_iota(jnp.int32, (PAIR, BLOCK), 1) - lax.broadcasted_iota(
         jnp.int32, (PAIR, BLOCK), 0
     )
@@ -183,34 +196,45 @@
     for q in range(6):
         col_stats[0, q:q + 1, :] = merged[:, q * LANES:(q + 1) * LANES]
 
+    col_offsets = [(d, other) for d in ORDER for other in (0, 1) if (d, other) != (0, 0)]
+    row_offsets = [(a, b) for a in (2, 1, 3, 0) for b in (2, 1, 3, 0) if (a, b) != (0, 0)]
+    row_offsets.sort(key=lambda ab: -min(ab[0], 4 - ab[0]) - min(ab[1], 4 - ab[1]))
+
     def col_peer(i):
-        return (r, (c + i) % COLS)
+        d, other = col_offsets[i]
+        return (r, z_of(d) * 2 + (k + other) % 2)
 
     def row_peer(i):
-        return ((r + i) % ROWS, c)
+        a, b = row_offsets[i]
+        return (line((a_pos + a) % 4, (b_pos + b) % 4), c)
+
+    def send_to(ref, sem, peer, i):
+        copy(
+            ref.at[0], ref.at[i + 1], stat_sem.at[2 * sem], stat_sem.at[2 * sem + 1], peer(i)
+        ).start()
 
     def spread(ref, sem, peer):
-        for i in range(1, 16):
-            copy(ref.at[0], ref.at[i], stat_sem.at[2 * sem], stat_sem.at[2 * sem + 1], peer(i)).start()
+        for i in range(15):
+            send_to(ref, sem, peer, i)
 
     def others(ref, sem):
         return pltpu.make_async_copy(ref.at[1:16], ref.at[1:16], stat_sem.at[sem])
 
-    spread(row_stats, 0, col_peer)
-    spread(col_stats, 1, row_peer)
+    def combine(every):
+        most = jnp.max(every, axis=0)
+        return most + jnp.log2(jnp.sum(jnp.exp2(every - most[None]), axis=0))
+
+    for i in range(15):
+        send_to(row_stats, 0, col_peer, i)
+        send_to(col_stats, 1, row_peer, i)
     for s in range(ZS):
         block = logits[s * PAIR:(s + 1) * PAIR, :]
         diagonal = diagonal + jnp.sum(jnp.where(own_pairs(s), block, 0.0), axis=0, keepdims=True)
     others(row_stats, 1).wait()
     others(col_stats, 3).wait()
 
-    def merge(stats):
-        every = stats[...]
-        most = jnp.max(every, axis=0)
-        return most + jnp.log2(jnp.sum(jnp.exp2(every - most[None]), axis=0))
-
-    row_merged[...] = merge(row_stats)
-    col_lse = merge(col_stats)
+    row_merged[...] = combine(row_stats[...])
+    col_lse = combine(col_stats[...])
     ordered = jnp.concatenate([row_merged[pl.ds(z_of(d), 1), :] for d in ORDER], axis=0)
     lse_columns = ordered.T
     col_row = jnp.concatenate([col_lse[q:q + 1, :] for q in range(6)], axis=1)
@@ -223,25 +247,28 @@
         pending.append(cp)
         return cp
 
-    swaps = []
-    for t in range(4):
+    def gradient_of(t):
         for s in (2 * t, 2 * t + 1):
             rows = slice(s * PAIR, (s + 1) * PAIR)
             block = logits[rows, :]
             total = jnp.exp2(block - lse_columns[0:PAIR, s:s + 1]) + jnp.exp2(block - col_row)
             total = total - jnp.where(own_pairs(s), 2.0, 0.0)
             dlogits[rows, :] = (0.5 * total).astype(BF16)
-        part = jnp.dot(
+
+    swaps = {}
+
+    def image_terms(t):
+        part = scale * jnp.dot(
             dlogits[2 * t * PAIR:(2 * t + 2) * PAIR, :], text_all[...], preferred_element_type=F32
         )
         image_part[2 * t:2 * t + 2] = part.astype(BF16).reshape(2, 2, SHARD, WIDTH)
-        swaps.append(reduce(
+        swaps[t] = reduce(
             image_part.at[2 * t:2 * t + 2, 1 - k], image_other.at[2 * t:2 * t + 2], 12 + t, sibling
-        ))
+        )
 
     def text_terms(h):
         rows = slice(h * HALF, (h + 1) * HALF)
-        part = lax.dot_general(
+        part = scale * lax.dot_general(
             dlogits[:, rows], image_all[...], (((0,), (0,)), ((), ())), preferred_element_type=F32
         )
         text_part[rows, :] = part.astype(BF16)
@@ -257,27 +284,28 @@
     quarter = {}
     far = {}
     direct = {}
+    gradient_of(0)
+    image_terms(0)
+    gradient_of(1)
+    image_terms(1)
+    gradient_of(2)
+    gradient_of(3)
     text_terms(0)
     swaps[0].wait_recv()
+    swaps[1].wait_recv()
+    for s, sign in sides:
+        far[sign] = reduce(summed(3 * sign), image_far.at[s], 3 + s, up(sign))
     block = summed(4)
-    for s, sign in ((0, 1), (1, -1)):
+    for s, sign in sides:
         quarter[sign] = reduce(half_of(block, s), image_half.at[s], 1 + s, up(2 * sign))
-    far[1] = reduce(summed(3), image_far.at[0], 3, up(1))
     text_terms(1)
     lines = {}
-    for b in (2, 1, 3):
-        for a in range(4):
+    for a in (2, 1, 3, 0):
+        for b in (2, 1, 3):
             lines[a, b] = reduce(
-                text_rows_of(text_part, line(a, (b_pos + b) % 4)), text_line.at[b - 1, a],
-                16 + 4 * b + a, on_b(b),
+                text_rows_of(text_part, line((a_pos + a) % 4, (b_pos + b) % 4)),
+                text_line.at[b - 1, a], 16 + 4 * b + a, on_b(b),
             )
-    swaps[1].wait_recv()
-    far[-1] = reduce(summed(-3), image_far.at[1], 4, up(-1))
-    swaps[2].wait_recv()
-    direct[1] = reduce(summed(1), image_near.at[0], 5, up(1))
-    swaps[3].wait_recv()
-    direct[-1] = reduce(summed(-1), image_near.at[1], 6, up(-1))
-
     col_total = jnp.sum(col_lse[0:6, :], axis=0, keepdims=True)
     on_block = jnp.sum(diagonal, axis=1, keepdims=True)
     loss_a[0] = jnp.concatenate(
@@ -285,33 +313,45 @@
     )
     spread(loss_a, 2, col_peer)
 
-    hop = {}
-    for s, sign in ((0, 1), (1, -1)):
-        far[sign].wait_recv()
-        quarter[sign].wait_recv()
-        both = of_z(2 * sign) + image_far[s].astype(F32)
-        cols = slice(s * HALF, (s + 1) * HALF)
-        rest = slice((1 - s) * HALF, (2 - s) * HALF)
-        slot = image_sum.at[SLOT[2 * sign]]
-        slot[:, rest] = both[:, rest].astype(BF16)
-        slot[:, cols] = (both[:, cols] + image_half[s].astype(F32)).astype(BF16)
-        hop[sign] = reduce(slot, image_hop.at[s], 7 + s, up(2 * sign))
-
-    for cp in lines.values():
-        cp.wait_recv()
+    image_terms(2)
+    image_terms(3)
+    swaps[2].wait_recv()
+    direct[1] = reduce(summed(1), image_near.at[0], 5, up(1))
+    swaps[3].wait_recv()
+    direct[-1] = reduce(summed(-1), image_near.at[1], 6, up(-1))
 
     def of_line(a):
-        index = (a_pos + a) % 4
-        total = text_rows_of(text_part, line(index, b_pos))[...].astype(F32)
+        for b in (1, 2, 3):
+            lines[a, b].wait_recv()
+        total = text_rows_of(text_part, line((a_pos + a) % 4, b_pos))[...].astype(F32)
         for b in range(3):
-            total = total + text_line[b, index].astype(F32)
+            total = total + text_line[b, a].astype(F32)
         return total
 
     last = {}
-    for a in (2, 1, 3):
+
+    def pass_line(a):
         text_hop[a] = of_line(a).astype(BF16)
         last[a] = reduce(text_hop.at[a], text_near.at[a], 8 + a, on_a(a))
 
+    hop = {}
+
+    def pass_sum(sign, s, half, early):
+        cols = slice(half * HALF, (half + 1) * HALF)
+        at = SLOT[2 * sign]
+        both = image_part[at, k, :, cols].astype(F32) + image_other[at, :, cols].astype(F32)
+        both = both + image_far[s, :, cols].astype(F32)
+        if not early:
+            both = both + image_half[s].astype(F32)
+        image_sum[at, :, cols] = both.astype(BF16)
+        hop[sign, early] = reduce(
+            image_sum.at[at, :, cols], image_hop.at[s, :, cols], 7 + s if early else 17 + s, up(2 * sign)
+        )
+
+    for s, sign in sides:
+        far[sign].wait_recv()
+        pass_sum(sign, s, 1 - s, True)
+    pass_line(2)
     others(loss_a, 5).wait()
     sums = jnp.sum(loss_a[...], axis=0)
     row_total = jnp.sum(row_merged[:, 0:PAIR], axis=0, keepdims=True)
@@ -319,17 +359,25 @@
     loss_b[0] = jnp.broadcast_to(row_total, (8, LANES))
     spread(loss_b, 3, row_peer)
 
+    for s, sign in sides:
+        quarter[sign].wait_recv()
+        pass_sum(sign, s, s, False)
+    pass_line(1)
+
+    pass_line(3)
+
     def project(unit_ref, inv_ref, gradient):
         unit = unit_ref[...]
         along = jnp.sum(unit * gradient, axis=1, keepdims=True)
         return inv_ref[:, 0:1] * (gradient - unit * along)
 
     gradient = of_z(0)
-    for s, sign in ((0, 1), (1, -1)):
+    for s, sign in sides:
         direct[sign].wait_recv()
         gradient = gradient + image_near[s].astype(F32)
-    for s, sign in ((0, 1), (1, -1)):
-        hop[sign].wait_recv()
+    for s, sign in sides:
+        hop[sign, True].wait_recv()
+        hop[sign, False].wait_recv()
         gradient = gradient + image_hop[s].astype(F32)
     grad_image_ref[...] = project(image_unit, image_inv, gradient)
 
@@ -394,8 +442,8 @@
             pltpu.VMEM((4, SHARD, WIDTH), BF16),
             pltpu.VMEM((4, SHARD, WIDTH), BF16),
             pltpu.SemaphoreType.DMA((2,)),
-            pltpu.SemaphoreType.DMA((40,)),
-            pltpu.SemaphoreType.DMA((40,)),
+            pltpu.SemaphoreType.DMA((42,)),
+            pltpu.SemaphoreType.DMA((42,)),
             pltpu.SemaphoreType.DMA((8,)),
             pltpu.SemaphoreType.DMA((32,)),
             pltpu.SemaphoreType.DMA((32,)),
@@ -404,8 +452,7 @@
             collective_id=0, has_side_effects=True, vmem_limit_bytes=60 << 20
         ),
     )(image_embed, text_embed, logit_scale)
-    scale = logit_scale[0]
-    return loss[0, 0], scale * grad_image, scale * grad_text
+    return loss[0, 0], grad_image, grad_text
 
 
 def solution(mesh):

time: 55.7 us -> 52 us (0.934)
  Pallas kernels: 50.7 us -> 46.5 us
  local copies, waits for them, and re-layouts: 0.6 us -> 2.88 us
  other arithmetic: 1.71 us -> 0 us
    pallas_call x1, Pallas kernels: 50.7 us -> 46.5 us  [body(): pl.pallas_call(kernel, name='contrastive', out_shape=(jax.ShapeDtypeStruc...]
    unnamed x2 -> x6, local copies, waits for them, and re-layouts: 0.6 us -> 2.88 us
    mul x1 -> x0, other arithmetic: 1.71 us -> none  [body(): return (loss[0, 0], scale * grad_image, scale * grad_text)]
where the time goes in v3:
time: 52 us; the launch traced here: 51.8 us
  Pallas kernels  46.5 us (89%)
  local copies, waits for them, and re-layouts  2.88 us (6%)
  between operations  2.47 us (5%)
    pallas_call x1, Pallas kernels, body(): pl.pallas_call(kernel, name='contrastive', out_shape=(jax.ShapeDtypeStruc...  46.5 us
    unnamed x6, local copies, waits for them, and re-layouts  2.88 us

profile of v3, /device:TPU:1, one launch (start us, length us, event | category | flops | bytes accessed | tf_op | source)
XLA Modules:
  0.0 51.8 jit_solution(11612406264761035609)
XLA Ops:
  1.3 46.5 %contrastive.1 = (f32[1,128]{1,0:T(1,128)}, f32[48,768]{1,0:T(8,128)}, f32[48,768]{1,0:T(8,128)}) custom-call(f32[48,768]{1,0:T(8,128)} %image_hbm.1, f32[48,768]{1,0:T(8,128)} %text_hbm.1, f32[1]{0:T(128)S(6)} %copy.9.scale_ref), custom_call_target="tpu_custom_call" | custom-call | tf_op jit(solution)/shard_map/contrastive/pallas_call | solution.py:404
  47.8 0.0 copy-start.1
  47.8 0.6 %copy-done.1 = f32[1,128]{1,0:T(1,128)S(1)} copy-done((f32[1,128]{1,0:T(1,128)S(1)}, f32[1,128]{1,0:T(1,128)}, u32[]{:S(2)}) %copy-start.1) | copy-done | bytes 536
  48.4 0.0 copy-start
  48.4 1.6 %copy.11 = f32[48,768]{1,0:T(8,128)} copy(f32[48,768]{1,0:T(8,128)} %get-tuple-element.13) | data formatting | bytes 294912
  50.0 0.0 copy-done
  50.0 0.7 %copy.12 = f32[48,768]{1,0:T(8,128)} copy(f32[48,768]{1,0:T(8,128)S(1)} %copy-done) | data formatting | bytes 294912
Async XLA Ops:
  47.8 0.6 %copy-start.1 = (f32[1,128]{1,0:T(1,128)S(1)}, f32[1,128]{1,0:T(1,128)}, u32[]{:S(2)}) copy-start(f32[1,128]{1,0:T(1,128)} %get-tuple-element.6) | copy-start | bytes 1540
  48.4 1.6 %copy-start = (f32[48,768]{1,0:T(8,128)S(1)}, f32[48,768]{1,0:T(8,128)}, u32[]{:S(2)}) copy-start(f32[48,768]{1,0:T(8,128)} %get-tuple-element.14) | copy-start | bytes 442372

commit v4 on v3

--- a/solution.py
+++ b/solution.py
@@ -352,6 +352,9 @@
         far[sign].wait_recv()
         pass_sum(sign, s, 1 - s, True)
     pass_line(2)
+    for s, sign in sides:
+        quarter[sign].wait_recv()
+        pass_sum(sign, s, s, False)
     others(loss_a, 5).wait()
     sums = jnp.sum(loss_a[...], axis=0)
     row_total = jnp.sum(row_merged[:, 0:PAIR], axis=0, keepdims=True)
@@ -359,9 +362,6 @@
     loss_b[0] = jnp.broadcast_to(row_total, (8, LANES))
     spread(loss_b, 3, row_peer)
 
-    for s, sign in sides:
-        quarter[sign].wait_recv()
-        pass_sum(sign, s, s, False)
     pass_line(1)
 
     pass_line(3)
@@ -449,9 +449,13 @@
             pltpu.SemaphoreType.DMA((32,)),
         ],
         compiler_params=pltpu.CompilerParams(
-            collective_id=0, has_side_effects=True, vmem_limit_bytes=60 << 20
+            collective_id=0, has_side_effects=True, vmem_limit_bytes=32 << 20
         ),
-    )(image_embed, text_embed, logit_scale)
+    )(
+        pltpu.with_memory_space_constraint(image_embed, pltpu.HBM),
+        pltpu.with_memory_space_constraint(text_embed, pltpu.HBM),
+        logit_scale,
+    )
     return loss[0, 0], grad_image, grad_text
 
 

time: 52 us -> 49.7 us (0.956)
  local copies, waits for them, and re-layouts: 2.88 us -> 1.32 us
  Pallas kernels: 46.5 us -> 45.8 us
    unnamed x6 -> x2, local copies, waits for them, and re-layouts: 2.88 us -> 1.32 us
    pallas_call x1, Pallas kernels: 46.5 us -> 45.8 us  [body(): pl.pallas_call(kernel, name='contrastive', out_shape=(jax.ShapeDtypeStruc...]
where the time goes in v4:
time: 49.7 us; the launch traced here: 49.5 us
  Pallas kernels  45.8 us (92%)
  between operations  2.45 us (5%)
  local copies, waits for them, and re-layouts  1.32 us (3%)
    pallas_call x1, Pallas kernels, body(): pl.pallas_call(kernel, name='contrastive', out_shape=(jax.ShapeDtypeStruc...  45.8 us
    unnamed x2, local copies, waits for them, and re-layouts  1.32 us

profile of v4, /device:TPU:1, one launch (start us, length us, event | category | flops | bytes accessed | tf_op | source)
XLA Modules:
  0.0 49.5 jit_solution(10845792042440734656)
XLA Ops:
  1.3 45.8 %contrastive.1 = (f32[1,128]{1,0:T(1,128)S(1)}, f32[48,768]{1,0:T(8,128)S(1)}, f32[48,768]{1,0:T(8,128)S(1)}) custom-call(f32[48,768]{1,0:T(8,128)} %image_hbm.1, f32[48,768]{1,0:T(8,128)} %text_hbm.1, f32[1]{0:T(128)S(6)} %copy.9.scale_ref), custom_call_target="tpu_custom_call" | custom-call | tf_op jit(solution)/shard_map/contrastive/pallas_call | solution.py:404
  47.1 0.7 %copy.11 = f32[48,768]{1,0:T(8,128)} copy(f32[48,768]{1,0:T(8,128)S(1)} %get-tuple-element.13) | data formatting | bytes 294912
  47.8 0.7 %copy.12 = f32[48,768]{1,0:T(8,128)} copy(f32[48,768]{1,0:T(8,128)S(1)} %get-tuple-element.14) | data formatting | bytes 294912

commit v5 on v4

--- a/solution.py
+++ b/solution.py
@@ -22,10 +22,10 @@
 def kernel(
     image_hbm, text_hbm, scale_ref, loss_ref, grad_image_ref, grad_text_ref,
     image_unit, text_unit, image_inv, text_inv, image_all, text_all, logits, col_parts, dlogits,
-    row_stats, col_stats, row_merged, loss_a, loss_b,
+    row_stats, col_stats, row_merged, loss_pair, loss_a, loss_b,
     image_part, image_other, image_sum, image_hop, image_far, image_half, image_near,
     text_part, text_line, text_hop, text_near,
-    in_sem, gather_send, gather_recv, stat_sem, reduce_send, reduce_recv,
+    in_sem, gather_send, gather_recv, stat_sem, pair_sem, reduce_send, reduce_recv,
 ):
     r = lax.axis_index("row")
     c = lax.axis_index("col")
@@ -107,17 +107,17 @@
     near = {}
     across = []
     ends = []
+    loads[1].wait()
+    text_own = text_rows(r)
+    text_own[...] = normalise(text_unit, text_inv)
+    for a in (1, 3, 2):
+        near[a] = gather(text_own, text_own, 16 + a, on_a(a))
     for turn in range(2):
         for s, sign in sides:
             h = (s + turn) % 2
             ahead[turn, sign] = gather(
                 half_of(image_rows(0), h), half_of(image_rows(-2 * sign), h), 4 * s + turn, up(2 * sign)
             )
-    loads[1].wait()
-    text_own = text_rows(r)
-    text_own[...] = normalise(text_unit, text_inv)
-    for a in (1, 3, 2):
-        near[a] = gather(text_own, text_own, 16 + a, on_a(a))
     for s, sign in sides:
         hops[sign] = gather(image_rows(0), image_rows(-sign), 4 * s + 2, up(sign))
 
@@ -230,6 +230,8 @@
     for s in range(ZS):
         block = logits[s * PAIR:(s + 1) * PAIR, :]
         diagonal = diagonal + jnp.sum(jnp.where(own_pairs(s), block, 0.0), axis=0, keepdims=True)
+    for cp in started:
+        cp.wait_send()
     others(row_stats, 1).wait()
     others(col_stats, 3).wait()
 
@@ -238,6 +240,14 @@
     ordered = jnp.concatenate([row_merged[pl.ds(z_of(d), 1), :] for d in ORDER], axis=0)
     lse_columns = ordered.T
     col_row = jnp.concatenate([col_lse[q:q + 1, :] for q in range(6)], axis=1)
+
+    col_total = jnp.sum(col_lse[0:6, :], axis=0, keepdims=True)
+    on_block = jnp.sum(diagonal, axis=1, keepdims=True)
+    loss_pair[0] = jnp.concatenate(
+        [col_total, jnp.broadcast_to(on_block, (1, LANES)), jnp.zeros((6, LANES), F32)], axis=0
+    )
+    pair = copy(loss_pair.at[0], loss_pair.at[1], pair_sem.at[0], pair_sem.at[1], sibling)
+    pair.start()
 
     pending = []
 
@@ -291,13 +301,6 @@
     gradient_of(2)
     gradient_of(3)
     text_terms(0)
-    swaps[0].wait_recv()
-    swaps[1].wait_recv()
-    for s, sign in sides:
-        far[sign] = reduce(summed(3 * sign), image_far.at[s], 3 + s, up(sign))
-    block = summed(4)
-    for s, sign in sides:
-        quarter[sign] = reduce(half_of(block, s), image_half.at[s], 1 + s, up(2 * sign))
     text_terms(1)
     lines = {}
     for a in (2, 1, 3, 0):
@@ -306,13 +309,21 @@
                 text_rows_of(text_part, line((a_pos + a) % 4, (b_pos + b) % 4)),
                 text_line.at[b - 1, a], 16 + 4 * b + a, on_b(b),
             )
-    col_total = jnp.sum(col_lse[0:6, :], axis=0, keepdims=True)
-    on_block = jnp.sum(diagonal, axis=1, keepdims=True)
-    loss_a[0] = jnp.concatenate(
-        [col_total, jnp.broadcast_to(on_block, (1, LANES)), jnp.zeros((6, LANES), F32)], axis=0
-    )
-    spread(loss_a, 2, col_peer)
-
+    pair.wait_recv()
+    loss_a[0] = jnp.sum(loss_pair[...], axis=0)
+    for i in range(1, ZS):
+        copy(loss_a.at[0], loss_a.at[i], stat_sem.at[4], stat_sem.at[5], up(i)).start()
+
+    def loss_z(sem):
+        return pltpu.make_async_copy(loss_a.at[1:ZS], loss_a.at[1:ZS], stat_sem.at[sem])
+
+    swaps[0].wait_recv()
+    swaps[1].wait_recv()
+    for s, sign in sides:
+        far[sign] = reduce(summed(3 * sign), image_far.at[s], 3 + s, up(sign))
+    block = summed(4)
+    for s, sign in sides:
+        quarter[sign] = reduce(half_of(block, s), image_half.at[s], 1 + s, up(2 * sign))
     image_terms(2)
     image_terms(3)
     swaps[2].wait_recv()
@@ -348,23 +359,32 @@
             image_sum.at[at, :, cols], image_hop.at[s, :, cols], 7 + s if early else 17 + s, up(2 * sign)
         )
 
-    for s, sign in sides:
-        far[sign].wait_recv()
-        pass_sum(sign, s, 1 - s, True)
-    pass_line(2)
-    for s, sign in sides:
-        quarter[sign].wait_recv()
-        pass_sum(sign, s, s, False)
-    others(loss_a, 5).wait()
+    loss_z(5).wait()
     sums = jnp.sum(loss_a[...], axis=0)
     row_total = jnp.sum(row_merged[:, 0:PAIR], axis=0, keepdims=True)
     row_total = jnp.sum(row_total, axis=1, keepdims=True) - 2.0 * sums[1:2, 0:1]
     loss_b[0] = jnp.broadcast_to(row_total, (8, LANES))
     spread(loss_b, 3, row_peer)
 
+    for s, sign in sides:
+        far[sign].wait_recv()
+        pass_sum(sign, s, 1 - s, True)
+    pass_line(2)
+    for s, sign in sides:
+        quarter[sign].wait_recv()
+        pass_sum(sign, s, s, False)
     pass_line(1)
 
     pass_line(3)
+
+    late = list(last.values()) + list(hop.values())
+    for cp in pending:
+        if all(cp is not other for other in late):
+            cp.wait_send()
+    for sem, ref in ((0, row_stats), (1, col_stats)):
+        others(ref, 2 * sem).wait()
+    pair.wait_send()
+    loss_z(4).wait()
 
     def project(unit_ref, inv_ref, gradient):
         unit = unit_ref[...]
@@ -390,10 +410,9 @@
     others(loss_b, 7).wait()
     total = jnp.sum(sums[0:1, :], axis=1, keepdims=True) + jnp.sum(loss_b[...], axis=0)[0:1, 0:1]
     loss_ref[...] = jnp.broadcast_to(total * (LN2 / (2.0 * ROWS * BLOCK)), (1, LANES))
-    for cp in started + pending:
+    others(loss_b, 6).wait()
+    for cp in list(last.values()) + list(hop.values()):
         cp.wait_send()
-    for sem, ref in enumerate((row_stats, col_stats, loss_a, loss_b)):
-        others(ref, 2 * sem).wait()
 
 
 def text_rows_of(ref, index):
@@ -428,7 +447,8 @@
             pltpu.VMEM((16, 8, LANES), F32),
             pltpu.VMEM((16, 8, LANES), F32),
             pltpu.VMEM((8, LANES), F32),
-            pltpu.VMEM((16, 8, LANES), F32),
+            pltpu.VMEM((2, 8, LANES), F32),
+            pltpu.VMEM((ZS, 8, LANES), F32),
             pltpu.VMEM((16, 8, LANES), F32),
             pltpu.VMEM((ZS, 2, SHARD, WIDTH), BF16),
             pltpu.VMEM((ZS, SHARD, WIDTH), BF16),
@@ -445,6 +465,7 @@
             pltpu.SemaphoreType.DMA((42,)),
             pltpu.SemaphoreType.DMA((42,)),
             pltpu.SemaphoreType.DMA((8,)),
+            pltpu.SemaphoreType.DMA((2,)),
             pltpu.SemaphoreType.DMA((32,)),
             pltpu.SemaphoreType.DMA((32,)),
         ],

time: 49.7 us -> 48.5 us (0.976)
  Pallas kernels: 45.8 us -> 44.7 us
    pallas_call x1, Pallas kernels: 45.8 us -> 44.7 us  [body(): pl.pallas_call(kernel, name='contrastive', out_shape=(jax.ShapeDtypeStruc...]
where the time goes in v5:
time: 48.5 us; the launch traced here: 48.4 us
  Pallas kernels  44.7 us (92%)
  between operations  2.45 us (5%)
  local copies, waits for them, and re-layouts  1.32 us (3%)
    pallas_call x1, Pallas kernels, body(): pl.pallas_call(kernel, name='contrastive', out_shape=(jax.ShapeDtypeStruc...  44.7 us
    unnamed x2, local copies, waits for them, and re-layouts  1.32 us

profile of v5, /device:TPU:1, one launch (start us, length us, event | category | flops | bytes accessed | tf_op | source)
XLA Modules:
  0.0 48.4 jit_solution(435778438808554373)
XLA Ops:
  1.3 44.7 %contrastive.1 = (f32[1,128]{1,0:T(1,128)S(1)}, f32[48,768]{1,0:T(8,128)S(1)}, f32[48,768]{1,0:T(8,128)S(1)}) custom-call(f32[48,768]{1,0:T(8,128)} %image_hbm.1, f32[48,768]{1,0:T(8,128)} %text_hbm.1, f32[1]{0:T(128)S(6)} %copy.9.scale_ref), custom_call_target="tpu_custom_call" | custom-call | tf_op jit(solution)/shard_map/contrastive/pallas_call | solution.py:423
  46.0 0.7 %copy.11 = f32[48,768]{1,0:T(8,128)} copy(f32[48,768]{1,0:T(8,128)S(1)} %get-tuple-element.13) | data formatting | bytes 294912
  46.6 0.7 %copy.12 = f32[48,768]{1,0:T(8,128)} copy(f32[48,768]{1,0:T(8,128)S(1)} %get-tuple-element.14) | data formatting | bytes 294912

commit v6 on v5

--- a/solution.py
+++ b/solution.py
@@ -82,7 +82,6 @@
         return unit.astype(BF16)
 
     row_stats[0] = jnp.zeros((8, LANES), F32)
-    col_stats[0] = jnp.zeros((8, LANES), F32)
     loads[0].wait()
     image_rows(0)[...] = normalise(image_unit, image_inv)
     pl.semaphore_wait(barrier, len(partners))
@@ -144,10 +143,10 @@
     pass_image(0)
     near[2].wait_recv()
     pass_text(2)
+    pass_image(1)
     for s, sign in sides:
         hops[sign].wait_recv()
         shares.append(share(-sign, 9 + s))
-    pass_image(1)
     for s, sign in sides:
         shares.append(share(-2 * sign, 11 + s))
     for cp in ends:
@@ -359,6 +358,10 @@
             image_sum.at[at, :, cols], image_hop.at[s, :, cols], 7 + s if early else 17 + s, up(2 * sign)
         )
 
+    for s, sign in sides:
+        far[sign].wait_recv()
+        pass_sum(sign, s, 1 - s, True)
+    pass_line(2)
     loss_z(5).wait()
     sums = jnp.sum(loss_a[...], axis=0)
     row_total = jnp.sum(row_merged[:, 0:PAIR], axis=0, keepdims=True)
@@ -366,10 +369,6 @@
     loss_b[0] = jnp.broadcast_to(row_total, (8, LANES))
     spread(loss_b, 3, row_peer)
 
-    for s, sign in sides:
-        far[sign].wait_recv()
-        pass_sum(sign, s, 1 - s, True)
-    pass_line(2)
     for s, sign in sides:
         quarter[sign].wait_recv()
         pass_sum(sign, s, s, False)
@@ -445,7 +444,7 @@
             pltpu.VMEM((ZS, BLOCK), F32),
             pltpu.VMEM((BLOCK, BLOCK), BF16),
             pltpu.VMEM((16, 8, LANES), F32),
-            pltpu.VMEM((16, 8, LANES), F32),
+            pltpu.VMEM((16, 6, LANES), F32),
             pltpu.VMEM((8, LANES), F32),
             pltpu.VMEM((2, 8, LANES), F32),
             pltpu.VMEM((ZS, 8, LANES), F32),

time: 48.5 us -> 48.5 us (level)
  no operation moved by 1% of the time
where the time goes in v6:
time: 48.5 us; the launch traced here: 48.4 us
  Pallas kernels  44.7 us (92%)
  between operations  2.45 us (5%)
  local copies, waits for them, and re-layouts  1.32 us (3%)
    pallas_call x1, Pallas kernels, body(): pl.pallas_call(kernel, name='contrastive', out_shape=(jax.ShapeDtypeStruc...  44.7 us
    unnamed x2, local copies, waits for them, and re-layouts  1.32 us

profile of v6, /device:TPU:1, one launch (start us, length us, event | category | flops | bytes accessed | tf_op | source)
XLA Modules:
  0.0 48.4 jit_solution(7069513771718189161)
XLA Ops:
  1.3 44.7 %contrastive.1 = (f32[1,128]{1,0:T(1,128)S(1)}, f32[48,768]{1,0:T(8,128)S(1)}, f32[48,768]{1,0:T(8,128)S(1)}) custom-call(f32[48,768]{1,0:T(8,128)} %image_hbm.1, f32[48,768]{1,0:T(8,128)} %text_hbm.1, f32[1]{0:T(128)S(6)} %copy.9.scale_ref), custom_call_target="tpu_custom_call" | custom-call | tf_op jit(solution)/shard_map/contrastive/pallas_call | solution.py:422
  46.0 0.7 %copy.11 = f32[48,768]{1,0:T(8,128)} copy(f32[48,768]{1,0:T(8,128)S(1)} %get-tuple-element.13) | data formatting | bytes 294912
  46.6 0.7 %copy.12 = f32[48,768]{1,0:T(8,128)} copy(f32[48,768]{1,0:T(8,128)S(1)} %get-tuple-element.14) | data formatting | bytes 294912
